TPU v7x, 32 devices: a whole 2x2x4 slice. The times are simulated.
32 devices in a mesh: section: 4 (over z), tm: 4 (over y, x), batch: 2 (over core).
Axes of the slice: x: 2, y: 2, z: 4, core: 2. Of those that a mesh axis runs over, the one named last changes fastest.
Arguments:
- acts: bfloat16 [4, 4, 8, 6, 10240], P('section', 'batch', 'tm'), may hold values from -6 to 6
- cot: bfloat16 [4, 8, 6, 10240], P('batch', 'tm'), may hold values from -6 to 6
- spatial_weight: bfloat16 [4, 9, 64, 64], P('section'), may hold values from -0.25 to 0.25
- temporal_weight: bfloat16 [4, 3, 64, 64], P('section'), may hold values from -0.4375 to 0.4375
Outputs:
- grad_in: bfloat16 [4, 4, 8, 6, 10240], P('section', 'batch', 'tm')
- grad_spatial: float32 [4, 9, 64, 64], P('section')
- grad_temporal: float32 [4, 3, 64, 64], P('section')
All inputs are finite; a program needn't handle non-finite values.
Results may differ from a plain program's by a relative error of at most 0.012.
Values may be sent and summed in bfloat16 or wider, within the bound.
A program may use at most 128 MiB of HBM per device.

v0:
```python
import jax
import jax.numpy as jnp
from jax import lax
from jax.sharding import PartitionSpec as P

TIME_DILATION = 2


def from_behind(value, axis, steps):
    count = lax.axis_size(axis)
    first, last = (max(0, -steps), min(count, count - steps))
    return lax.ppermute(value, axis, [(source, source + steps) for source in range(first, last)])


def split_pixels(a, chans):
    return a.reshape(a.shape[:-1] + (a.shape[-1] // chans, chans))


def paired_kernel(kernel):
    return jnp.kron(jnp.eye(2, dtype=kernel.dtype), kernel)


def spatial_fwd(x, ws):
    rows, width = (x.shape[1], x.shape[2])
    chans = ws.shape[-1]
    padded = jnp.pad(x, ((0, 0), (1, 1), (chans, chans)))
    total = jnp.zeros(x.shape, jnp.float32)
    for i in range(3):
        for j in range(3):
            piece = split_pixels(padded[:, i : i + rows, j * chans : j * chans + width], 2 * chans)
            total = total + jnp.einsum(
                "nrpa,ab->nrpb",
                piece,
                paired_kernel(ws[3 * i + j]),
                preferred_element_type=jnp.float32,
            ).reshape(x.shape)
    return total


def spatial_back(gz, x, ws):
    rows, width = (x.shape[1], x.shape[2])
    chans = ws.shape[-1]
    xpad = jnp.pad(x, ((0, 0), (1, 1), (chans, chans)))
    gradient_padded = jnp.pad(gz, ((0, 0), (1, 1), (chans, chans)))
    gz_pairs = split_pixels(gz, 2 * chans)
    total = jnp.zeros(x.shape, jnp.float32)
    grads = []
    for i in range(3):
        for j in range(3):
            gpiece = split_pixels(
                gradient_padded[:, 2 - i : 2 - i + rows, (2 - j) * chans : (2 - j) * chans + width],
                2 * chans,
            )
            total = total + jnp.einsum(
                "nrpb,ab->nrpa",
                gpiece,
                paired_kernel(ws[3 * i + j]),
                preferred_element_type=jnp.float32,
            ).reshape(x.shape)
            xpiece = split_pixels(xpad[:, i : i + rows, j * chans : j * chans + width], 2 * chans)
            square = jnp.einsum(
                "nrpa,nrpb->ab", xpiece, gz_pairs, preferred_element_type=jnp.float32
            )
            grads.append(square[:chans, :chans] + square[chans:, chans:])
    return (total, jnp.stack(grads))


def temporal_back(h, gradient_piece, gradient_padded, dilation_step, wt):
    count = gradient_piece.shape[0]
    chans = wt.shape[-1]
    kernel_taps = [
        gradient_padded[2 * dilation_step : 2 * dilation_step + count],
        gradient_piece,
        gradient_padded[0:count],
    ]
    h_pix = split_pixels(h, chans)
    gh = jnp.zeros(gradient_piece.shape, jnp.float32)
    tgrads = []
    for k in range(3):
        tap = split_pixels(kernel_taps[k], chans)
        gh = gh + jnp.einsum(
            "trwd,cd->trwc", tap, wt[k], preferred_element_type=jnp.float32
        ).reshape(gradient_piece.shape)
        tgrads.append(jnp.einsum("trwc,trwd->cd", h_pix, tap, preferred_element_type=jnp.float32))
    return (gh.astype(jnp.bfloat16), jnp.stack(tgrads))


def section_backward(x, gradient_piece, ws, wt):
    dilation_step = TIME_DILATION
    z = spatial_fwd(x, ws)
    sig = jax.nn.sigmoid(z)
    h = (z * sig).astype(jnp.bfloat16)
    deriv = sig * (1.0 + z * (1.0 - sig))
    tile_gradient, h_tile = (
        lax.all_to_all(gradient_piece, "tm", split_axis=2, concat_axis=0, tiled=True),
        lax.all_to_all(h, "tm", split_axis=2, concat_axis=0, tiled=True),
    )
    gradient_padded = jnp.pad(tile_gradient, ((dilation_step, dilation_step), (0, 0), (0, 0)))
    gh_tile, tgrads = temporal_back(h_tile, tile_gradient, gradient_padded, dilation_step, wt)
    gh = lax.all_to_all(gh_tile, "tm", split_axis=0, concat_axis=2, tiled=True)
    gz = (gh.astype(jnp.float32) * deriv).astype(jnp.bfloat16)
    back, sgrads = spatial_back(gz, x, ws)
    result = (gradient_piece.astype(jnp.float32) + back).astype(jnp.bfloat16)
    return (result, sgrads, tgrads)


def body(acts, cot, spatial_weight, temporal_weight):
    section_idx = lax.axis_index("section")
    number_sections = lax.axis_size("section")
    micro = acts.shape[1]
    local_acts = acts[0]
    ws = spatial_weight[0]
    wt = temporal_weight[0]
    received = jnp.zeros(cot.shape[1:], jnp.bfloat16)
    grads_in = jnp.zeros(local_acts.shape, jnp.bfloat16)
    acc_spatial = jnp.zeros(ws.shape, jnp.float32)
    acc_temporal = jnp.zeros(wt.shape, jnp.float32)
    total_turns = micro + number_sections - 1
    for turn in range(total_turns):
        which = jnp.int32(turn) - (number_sections - 1 - section_idx)
        valid = jnp.logical_and(which >= 0, which < micro)
        clipped = jnp.clip(which, 0, micro - 1)
        x_now = lax.dynamic_index_in_dim(local_acts, clipped, 0, keepdims=False)
        top_grad = lax.dynamic_index_in_dim(cot, clipped, 0, keepdims=False)
        incoming = jnp.where(section_idx == number_sections - 1, top_grad, received)
        result, sgrads, tgrads = section_backward(x_now, incoming, ws, wt)
        weight = valid.astype(jnp.float32)
        acc_spatial = acc_spatial + weight * sgrads
        acc_temporal = acc_temporal + weight * tgrads
        select = (jnp.arange(micro, dtype=jnp.int32) == which)[:, None, None, None]
        grads_in = jnp.where(select, result[None], grads_in)
        if turn + 1 < total_turns:
            received = from_behind(result, "section", -1)
    sum_spatial, sum_temporal = lax.psum((acc_spatial, acc_temporal), ("tm", "batch"))
    return (grads_in[None], sum_spatial[None], sum_temporal[None])


def solution(mesh):
    in_specs = (
        P("section", "batch", "tm", None, None),
        P("batch", "tm", None, None),
        P("section", None, None, None),
        P("section", None, None, None),
    )
    out_specs = (
        P("section", "batch", "tm", None, None),
        P("section", None, None, None),
        P("section", None, None, None),
    )
    return jax.shard_map(body, mesh=mesh, in_specs=in_specs, out_specs=out_specs, check_vma=False)
```

profile of v0, /device:TPU:24, one launch (start us, length us, event | category | flops | bytes accessed | tf_op | source)
XLA Modules:
  0.0 929.5 jit_solution(14927379624928204376)
XLA Ops:
  8.3 8.2 copy.623
  16.6 10.0 %reshape.1685 = bf16[4,2,15360]{2,1,0:T(2,128)(2,1)} reshape(bf16[10240,2,6]{2,1,0:T(2,128)(2,1)} %bitcast.1159) | data formatting | bytes 491520
  26.5 4.2 all-to-all-start
  126.4 13.6 %reshape.1686 = bf16[10240,2,6]{2,1,0:T(2,128)(2,1)} reshape(bf16[4,2,15360]{2,1,0:T(2,128)(2,1)} %all-to-all-done) | data formatting | bytes 491520
  140.0 10.6 %copy.624 = bf16[2,6,4,2560]{3,0,2,1:T(2,128)(2,1)S(1)} copy(bf16[2,6,4,2560]{1,0,3,2:T(2,128)(2,1)} %bitcast.1160) | data formatting | bytes 491520 | tf_op jit(solution)/shard_map/all_to_all | solution.py:95
  153.7 4.3 all-to-all-start.1
  159.1 4.6 all-to-all-done.1
  205.2 10.3 %copy.809 = bf16[2,6,10240]{1,0,2:T(2,128)(2,1)} copy(bf16[2,6,10240]{2,0,1:T(2,128)(2,1)} %get-tuple-element.11) | data formatting | bytes 491520 | tf_op jit(solution)/shard_map/convert_element_type | solution.py:92
  215.5 9.9 %reshape.1695 = bf16[4,2,15360]{2,1,0:T(2,128)(2,1)} reshape(bf16[10240,2,6]{2,1,0:T(2,128)(2,1)} %bitcast.1161) | data formatting | bytes 491520
  233.9 8.2 copy.651
  242.1 9.9 %reshape.1687 = bf16[4,2,15360]{2,1,0:T(2,128)(2,1)} reshape(bf16[10240,2,6]{2,1,0:T(2,128)(2,1)} %bitcast.1175) | data formatting | bytes 491520
  257.1 12.6 %reshape.1696 = bf16[10240,2,6]{2,1,0:T(2,128)(2,1)} reshape(bf16[4,2,15360]{2,1,0:T(2,128)(2,1)S(1)} %all-to-all-done.10) | data formatting | bytes 491520
  269.7 12.2 %copy.902 = bf16[2,6,4,2560]{3,2,0,1:T(4,128)(2,1)S(1)} copy(bf16[2,6,4,2560]{1,0,3,2:T(2,128)(2,1)} %bitcast.1162) | data formatting | bytes 491520 | tf_op jit(solution)/shard_map/all_to_all | solution.py:96
  283.3 12.6 %reshape.1688 = bf16[10240,2,6]{2,1,0:T(2,128)(2,1)} reshape(bf16[4,2,15360]{2,1,0:T(2,128)(2,1)S(1)} %all-to-all-done.2) | data formatting | bytes 491520
  296.0 10.2 %copy.652 = bf16[2,6,4,2560]{3,0,2,1:T(2,128)(2,1)S(1)} copy(bf16[2,6,4,2560]{1,0,3,2:T(2,128)(2,1)} %bitcast.1163) | data formatting | bytes 491520 | tf_op jit(solution)/shard_map/all_to_all | solution.py:95
  314.8 4.4 all-to-all-start.3
  366.4 10.3 %copy.812 = bf16[2,6,10240]{1,0,2:T(2,128)(2,1)} copy(bf16[2,6,10240]{2,0,1:T(2,128)(2,1)} %get-tuple-element.9) | data formatting | bytes 491520 | tf_op jit(solution)/shard_map/convert_element_type | solution.py:92
  376.7 9.9 %reshape.1697 = bf16[4,2,15360]{2,1,0:T(2,128)(2,1)} reshape(bf16[10240,2,6]{2,1,0:T(2,128)(2,1)} %bitcast.1164) | data formatting | bytes 491520
  395.5 8.1 copy.679
  403.7 9.9 %reshape.1689 = bf16[4,2,15360]{2,1,0:T(2,128)(2,1)} reshape(bf16[10240,2,6]{2,1,0:T(2,128)(2,1)} %bitcast.1176) | data formatting | bytes 491520
  418.4 12.6 %reshape.1698 = bf16[10240,2,6]{2,1,0:T(2,128)(2,1)} reshape(bf16[4,2,15360]{2,1,0:T(2,128)(2,1)S(1)} %all-to-all-done.11) | data formatting | bytes 491520
  431.1 12.2 %copy.903 = bf16[2,6,4,2560]{3,2,0,1:T(4,128)(2,1)S(1)} copy(bf16[2,6,4,2560]{1,0,3,2:T(2,128)(2,1)} %bitcast.1165) | data formatting | bytes 491520 | tf_op jit(solution)/shard_map/all_to_all | solution.py:96
  444.7 12.6 %reshape.1690 = bf16[10240,2,6]{2,1,0:T(2,128)(2,1)} reshape(bf16[4,2,15360]{2,1,0:T(2,128)(2,1)S(1)} %all-to-all-done.4) | data formatting | bytes 491520
  457.3 10.2 %copy.680 = bf16[2,6,4,2560]{3,0,2,1:T(2,128)(2,1)S(1)} copy(bf16[2,6,4,2560]{1,0,3,2:T(2,128)(2,1)} %bitcast.1166) | data formatting | bytes 491520 | tf_op jit(solution)/shard_map/all_to_all | solution.py:95
  476.2 4.4 all-to-all-start.5
  525.7 10.2 %copy.815 = bf16[2,6,10240]{1,0,2:T(2,128)(2,1)} copy(bf16[2,6,10240]{2,0,1:T(2,128)(2,1)} %get-tuple-element.7) | data formatting | bytes 491520 | tf_op jit(solution)/shard_map/convert_element_type | solution.py:92
  536.0 9.9 %reshape.1699 = bf16[4,2,15360]{2,1,0:T(2,128)(2,1)} reshape(bf16[10240,2,6]{2,1,0:T(2,128)(2,1)} %bitcast.1167) | data formatting | bytes 491520
  554.6 8.1 copy.707
  562.8 9.9 %reshape.1691 = bf16[4,2,15360]{2,1,0:T(2,128)(2,1)} reshape(bf16[10240,2,6]{2,1,0:T(2,128)(2,1)} %bitcast.1177) | data formatting | bytes 491520
  577.8 12.6 %reshape.1700 = bf16[10240,2,6]{2,1,0:T(2,128)(2,1)} reshape(bf16[4,2,15360]{2,1,0:T(2,128)(2,1)S(1)} %all-to-all-done.12) | data formatting | bytes 491520
  590.4 12.2 %copy.904 = bf16[2,6,4,2560]{3,2,0,1:T(4,128)(2,1)S(1)} copy(bf16[2,6,4,2560]{1,0,3,2:T(2,128)(2,1)} %bitcast.1168) | data formatting | bytes 491520 | tf_op jit(solution)/shard_map/all_to_all | solution.py:96
  604.0 12.6 %reshape.1692 = bf16[10240,2,6]{2,1,0:T(2,128)(2,1)} reshape(bf16[4,2,15360]{2,1,0:T(2,128)(2,1)S(1)} %all-to-all-done.6) | data formatting | bytes 491520
  616.6 10.2 %copy.708 = bf16[2,6,4,2560]{3,0,2,1:T(2,128)(2,1)S(1)} copy(bf16[2,6,4,2560]{1,0,3,2:T(2,128)(2,1)} %bitcast.1169) | data formatting | bytes 491520 | tf_op jit(solution)/shard_map/all_to_all | solution.py:95
  635.5 4.6 all-to-all-start.7
  687.6 10.2 %copy.818 = bf16[2,6,10240]{1,0,2:T(2,128)(2,1)} copy(bf16[2,6,10240]{2,0,1:T(2,128)(2,1)} %get-tuple-element.5) | data formatting | bytes 491520 | tf_op jit(solution)/shard_map/convert_element_type | solution.py:92
  697.8 9.9 %reshape.1701 = bf16[4,2,15360]{2,1,0:T(2,128)(2,1)} reshape(bf16[10240,2,6]{2,1,0:T(2,128)(2,1)} %bitcast.1170) | data formatting | bytes 491520
  712.9 8.1 copy.735
  721.1 9.9 %reshape.1693 = bf16[4,2,15360]{2,1,0:T(2,128)(2,1)} reshape(bf16[10240,2,6]{2,1,0:T(2,128)(2,1)} %bitcast.1178) | data formatting | bytes 491520
  735.9 12.6 %reshape.1702 = bf16[10240,2,6]{2,1,0:T(2,128)(2,1)} reshape(bf16[4,2,15360]{2,1,0:T(2,128)(2,1)S(1)} %all-to-all-done.13) | data formatting | bytes 491520
  748.5 12.2 %copy.905 = bf16[2,6,4,2560]{3,2,0,1:T(4,128)(2,1)S(1)} copy(bf16[2,6,4,2560]{1,0,3,2:T(2,128)(2,1)} %bitcast.1171) | data formatting | bytes 491520 | tf_op jit(solution)/shard_map/all_to_all | solution.py:96
  762.1 12.6 %reshape.1694 = bf16[10240,2,6]{2,1,0:T(2,128)(2,1)} reshape(bf16[4,2,15360]{2,1,0:T(2,128)(2,1)S(1)} %all-to-all-done.8) | data formatting | bytes 491520
  774.7 10.2 %copy.736 = bf16[2,6,4,2560]{3,0,2,1:T(2,128)(2,1)S(1)} copy(bf16[2,6,4,2560]{1,0,3,2:T(2,128)(2,1)} %bitcast.1172) | data formatting | bytes 491520 | tf_op jit(solution)/shard_map/all_to_all | solution.py:95
  788.7 4.3 all-to-all-start.9
  841.1 10.3 %copy.821 = bf16[2,6,10240]{1,0,2:T(2,128)(2,1)} copy(bf16[2,6,10240]{2,0,1:T(2,128)(2,1)} %get-tuple-element.3) | data formatting | bytes 491520 | tf_op jit(solution)/shard_map/convert_element_type | solution.py:92
  851.4 9.9 %reshape.1703 = bf16[4,2,15360]{2,1,0:T(2,128)(2,1)} reshape(bf16[10240,2,6]{2,1,0:T(2,128)(2,1)} %bitcast.1173) | data formatting | bytes 491520
  870.4 12.6 %reshape.1704 = bf16[10240,2,6]{2,1,0:T(2,128)(2,1)} reshape(bf16[4,2,15360]{2,1,0:T(2,128)(2,1)S(1)} %all-to-all-done.14) | data formatting | bytes 491520
  883.2 12.3 %copy.906 = bf16[2,6,4,2560]{3,2,0,1:T(4,128)(2,1)S(1)} copy(bf16[2,6,4,2560]{1,0,3,2:T(2,128)(2,1)} %bitcast.1174) | data formatting | bytes 491520 | tf_op jit(solution)/shard_map/all_to_all | solution.py:96
  897.0 23.7 %psum.15 = f32[1,3,64,64]{3,2,1,0:T(8,128)} all-reduce(f32[1,3,64,64]{3,2,1,0:T(8,128)S(1)} %fusion.170), channel_id=1, replica_groups=mesh['section'=4,'tm'=4,'batch'=2] {'tm','batch'}, use_global_device_ids=true, to_apply=%region_1.2 | all-reduce | flops 12288 | bytes 98304 | tf_op jit(solution)/shard_map/psum | solution.py:134
  (812 shorter events, 426.2 us)
Async XLA Ops:
  26.5 99.9 %all-to-all-start = ((bf16[4,2,15360]{2,1,0:T(2,128)(2,1)}), bf16[4,2,15360]{2,1,0:T(2,128)(2,1)}, u32[]{:S(2)}, u32[]{:S(2)}) async-start(bf16[4,2,15360]{2,1,0:T(2,128)(2,1)} %reshape.1685), calls=%async_computation | async-start | bytes 491520 | tf_op jit(solution)/shard_map/all_to_all | solution.py:95
  33.8 160.6 %copy-start.16 = (bf16[128,128,1,1]{1,0,2,3:T(8,128)(2,1)}, bf16[128,128,1,1]{1,0,2,3:T(8,128)(2,1)S(1)}, u32[]{:S(2)}) copy-start(bf16[128,128,1,1]{1,0,2,3:T(8,128)(2,1)S(1)} %reshape.1603) | copy-start | bytes 98308
  33.9 160.8 %copy-start.11 = (bf16[128,128,1,1]{1,0,2,3:T(8,128)(2,1)}, bf16[128,128,1,1]{1,0,2,3:T(8,128)(2,1)S(1)}, u32[]{:S(2)}) copy-start(bf16[128,128,1,1]{1,0,2,3:T(8,128)(2,1)S(1)} %reshape.1604) | copy-start | bytes 98308
  34.1 160.9 %copy-start.6 = (bf16[128,128,1,1]{1,0,2,3:T(8,128)(2,1)}, bf16[128,128,1,1]{1,0,2,3:T(8,128)(2,1)S(1)}, u32[]{:S(2)}) copy-start(bf16[128,128,1,1]{1,0,2,3:T(8,128)(2,1)S(1)} %reshape.1605) | copy-start | bytes 98308
  34.2 162.0 %copy-start.1 = (bf16[128,128,1,1]{1,0,2,3:T(8,128)(2,1)}, bf16[128,128,1,1]{1,0,2,3:T(8,128)(2,1)S(1)}, u32[]{:S(2)}) copy-start(bf16[128,128,1,1]{1,0,2,3:T(8,128)(2,1)S(1)} %reshape.1606) | copy-start | bytes 98308
  34.6 159.6 %copy-start.21 = (bf16[128,128,1,1]{1,0,2,3:T(8,128)(2,1)}, bf16[128,128,1,1]{1,0,2,3:T(8,128)(2,1)S(1)}, u32[]{:S(2)}) copy-start(bf16[128,128,1,1]{1,0,2,3:T(8,128)(2,1)S(1)} %reshape.1602) | copy-start | bytes 98308
  35.7 90.1 %copy-start.43 = (bf16[2,6,80,128]{3,2,0,1:T(8,128)(2,1)}, bf16[2,6,80,128]{3,2,0,1:T(8,128)(2,1)S(1)}, u32[]{:S(2)}) copy-start(bf16[2,6,80,128]{3,2,0,1:T(8,128)(2,1)S(1)} %reshape.1505) | copy-start | bytes 737284
  153.7 9.9 %all-to-all-start.1 = ((bf16[8,6,2560]{2,1,0:T(8,128)(2,1)}), bf16[8,6,2560]{2,1,0:T(8,128)(2,1)S(1)}, u32[]{:S(2)}, u32[]{:S(2)}) async-start(bf16[8,6,2560]{2,1,0:T(8,128)(2,1)} %reshape.1671), calls=%async_computation.1 | async-start | bytes 655360 | tf_op jit(solution)/shard_map/all_to_all | solution.py:100
  202.7 31.0 %collective-permute-start = (bf16[2,6,10240]{2,0,1:T(2,128)(2,1)S(1)}, bf16[2,6,10240]{2,0,1:T(2,128)(2,1)S(1)}, u32[]{:S(2)}, u32[]{:S(2)}) collective-permute-start(bf16[2,6,10240]{2,0,1:T(2,128)(2,1)S(1)} %add_convert_fusion.5), channel_id=1, source_target_pairs={{8,0},{16,8},{24,16},{9,1},{17,9},{25,17},{10,2},{18,10},{26,18},{... | collective-permute-start | bytes 737288 | tf_op jit(solution)/shard_map/ppermute | solution.py:12
  205.1 25.1 %copy-start.162 = (f32[128,128]{1,0:T(8,128)S(1)}, f32[128,128]{1,0:T(8,128)}, u32[]{:S(2)}) copy-start(f32[128,128]{1,0:T(8,128)} %convolution_bitcast_fusion.41) | copy-start | bytes 196612
  205.1 25.7 %copy-start.158 = (f32[128,128]{1,0:T(8,128)S(1)}, f32[128,128]{1,0:T(8,128)}, u32[]{:S(2)}) copy-start(f32[128,128]{1,0:T(8,128)} %convolution_bitcast_fusion.40) | copy-start | bytes 196612
  205.1 26.4 %copy-start.154 = (f32[128,128]{1,0:T(8,128)S(1)}, f32[128,128]{1,0:T(8,128)}, u32[]{:S(2)}) copy-start(f32[128,128]{1,0:T(8,128)} %convolution_bitcast_fusion.39) | copy-start | bytes 196612
  205.1 27.1 %copy-start.150 = (f32[128,128]{1,0:T(8,128)S(1)}, f32[128,128]{1,0:T(8,128)}, u32[]{:S(2)}) copy-start(f32[128,128]{1,0:T(8,128)} %convolution_bitcast_fusion.38) | copy-start | bytes 196612
  205.1 27.8 %copy-start.149 = (f32[128,128]{1,0:T(8,128)S(1)}, f32[128,128]{1,0:T(8,128)}, u32[]{:S(2)}) copy-start(f32[128,128]{1,0:T(8,128)} %convolution_bitcast_fusion.37) | copy-start | bytes 196612
  225.4 26.6 %all-to-all-start.10 = ((bf16[4,2,15360]{2,1,0:T(2,128)(2,1)}), bf16[4,2,15360]{2,1,0:T(2,128)(2,1)S(1)}, u32[]{:S(2)}, u32[]{:S(2)}) async-start(bf16[4,2,15360]{2,1,0:T(2,128)(2,1)} %reshape.1695), calls=%async_computation.10 | async-start | bytes 491520 | tf_op jit(solution)/shard_map/all_to_all | solution.py:96
  252.0 31.3 %all-to-all-start.2 = ((bf16[4,2,15360]{2,1,0:T(2,128)(2,1)}), bf16[4,2,15360]{2,1,0:T(2,128)(2,1)S(1)}, u32[]{:S(2)}, u32[]{:S(2)}) async-start(bf16[4,2,15360]{2,1,0:T(2,128)(2,1)} %reshape.1687), calls=%async_computation.2 | async-start | bytes 491520 | tf_op jit(solution)/shard_map/all_to_all | solution.py:95
  314.8 10.0 %all-to-all-start.3 = ((bf16[8,6,2560]{2,1,0:T(8,128)(2,1)}), bf16[8,6,2560]{2,1,0:T(8,128)(2,1)}, u32[]{:S(2)}, u32[]{:S(2)}) async-start(bf16[8,6,2560]{2,1,0:T(8,128)(2,1)} %reshape.1681), calls=%async_computation.3 | async-start | bytes 655360 | tf_op jit(solution)/shard_map/all_to_all | solution.py:100
  364.0 31.2 %collective-permute-start.1 = (bf16[2,6,10240]{2,0,1:T(2,128)(2,1)S(1)}, bf16[2,6,10240]{2,0,1:T(2,128)(2,1)S(1)}, u32[]{:S(2)}, u32[]{:S(2)}) collective-permute-start(bf16[2,6,10240]{2,0,1:T(2,128)(2,1)S(1)} %add_convert_fusion.4), channel_id=1, source_target_pairs={{8,0},{16,8},{24,16},{9,1},{17,9},{25,17},{10,2},{18,10},{26,18},{... | collective-permute-start | bytes 737288 | tf_op jit(solution)/shard_map/ppermute | solution.py:12
  366.4 25.4 %copy-start.167 = (f32[128,128]{1,0:T(8,128)S(1)}, f32[128,128]{1,0:T(8,128)}, u32[]{:S(2)}) copy-start(f32[128,128]{1,0:T(8,128)} %convolution_bitcast_fusion.32) | copy-start | bytes 196612
  366.4 26.1 %copy-start.163 = (f32[128,128]{1,0:T(8,128)S(1)}, f32[128,128]{1,0:T(8,128)}, u32[]{:S(2)}) copy-start(f32[128,128]{1,0:T(8,128)} %convolution_bitcast_fusion.31) | copy-start | bytes 196612
  366.4 26.8 %copy-start.159 = (f32[128,128]{1,0:T(8,128)S(1)}, f32[128,128]{1,0:T(8,128)}, u32[]{:S(2)}) copy-start(f32[128,128]{1,0:T(8,128)} %convolution_bitcast_fusion.30) | copy-start | bytes 196612
  366.4 27.4 %copy-start.155 = (f32[128,128]{1,0:T(8,128)S(1)}, f32[128,128]{1,0:T(8,128)}, u32[]{:S(2)}) copy-start(f32[128,128]{1,0:T(8,128)} %convolution_bitcast_fusion.29) | copy-start | bytes 196612
  366.4 28.1 %copy-start.151 = (f32[128,128]{1,0:T(8,128)S(1)}, f32[128,128]{1,0:T(8,128)}, u32[]{:S(2)}) copy-start(f32[128,128]{1,0:T(8,128)} %convolution_bitcast_fusion.28) | copy-start | bytes 196612
  386.6 26.9 %all-to-all-start.11 = ((bf16[4,2,15360]{2,1,0:T(2,128)(2,1)}), bf16[4,2,15360]{2,1,0:T(2,128)(2,1)S(1)}, u32[]{:S(2)}, u32[]{:S(2)}) async-start(bf16[4,2,15360]{2,1,0:T(2,128)(2,1)} %reshape.1697), calls=%async_computation.11 | async-start | bytes 491520 | tf_op jit(solution)/shard_map/all_to_all | solution.py:96
  413.6 31.1 %all-to-all-start.4 = ((bf16[4,2,15360]{2,1,0:T(2,128)(2,1)}), bf16[4,2,15360]{2,1,0:T(2,128)(2,1)S(1)}, u32[]{:S(2)}, u32[]{:S(2)}) async-start(bf16[4,2,15360]{2,1,0:T(2,128)(2,1)} %reshape.1689), calls=%async_computation.4 | async-start | bytes 491520 | tf_op jit(solution)/shard_map/all_to_all | solution.py:95
  476.2 10.0 %all-to-all-start.5 = ((bf16[8,6,2560]{2,1,0:T(8,128)(2,1)}), bf16[8,6,2560]{2,1,0:T(8,128)(2,1)}, u32[]{:S(2)}, u32[]{:S(2)}) async-start(bf16[8,6,2560]{2,1,0:T(8,128)(2,1)} %reshape.1682), calls=%async_computation.5 | async-start | bytes 655360 | tf_op jit(solution)/shard_map/all_to_all | solution.py:100
  523.5 30.9 %collective-permute-start.2 = (bf16[2,6,10240]{2,0,1:T(2,128)(2,1)S(1)}, bf16[2,6,10240]{2,0,1:T(2,128)(2,1)S(1)}, u32[]{:S(2)}, u32[]{:S(2)}) collective-permute-start(bf16[2,6,10240]{2,0,1:T(2,128)(2,1)S(1)} %add_convert_fusion.3), channel_id=1, source_target_pairs={{8,0},{16,8},{24,16},{9,1},{17,9},{25,17},{10,2},{18,10},{26,18},{... | collective-permute-start | bytes 737288 | tf_op jit(solution)/shard_map/ppermute | solution.py:12
  525.7 25.2 %copy-start.169 = (f32[128,128]{1,0:T(8,128)S(1)}, f32[128,128]{1,0:T(8,128)}, u32[]{:S(2)}) copy-start(f32[128,128]{1,0:T(8,128)} %convolution_bitcast_fusion.23) | copy-start | bytes 196612
  525.7 25.9 %copy-start.165 = (f32[128,128]{1,0:T(8,128)S(1)}, f32[128,128]{1,0:T(8,128)}, u32[]{:S(2)}) copy-start(f32[128,128]{1,0:T(8,128)} %convolution_bitcast_fusion.22) | copy-start | bytes 196612
  525.7 26.6 %copy-start.161 = (f32[128,128]{1,0:T(8,128)S(1)}, f32[128,128]{1,0:T(8,128)}, u32[]{:S(2)}) copy-start(f32[128,128]{1,0:T(8,128)} %convolution_bitcast_fusion.21) | copy-start | bytes 196612
  525.7 27.2 %copy-start.157 = (f32[128,128]{1,0:T(8,128)S(1)}, f32[128,128]{1,0:T(8,128)}, u32[]{:S(2)}) copy-start(f32[128,128]{1,0:T(8,128)} %convolution_bitcast_fusion.20) | copy-start | bytes 196612
  525.7 27.9 %copy-start.153 = (f32[128,128]{1,0:T(8,128)S(1)}, f32[128,128]{1,0:T(8,128)}, u32[]{:S(2)}) copy-start(f32[128,128]{1,0:T(8,128)} %convolution_bitcast_fusion.19) | copy-start | bytes 196612
  545.9 26.8 %all-to-all-start.12 = ((bf16[4,2,15360]{2,1,0:T(2,128)(2,1)}), bf16[4,2,15360]{2,1,0:T(2,128)(2,1)S(1)}, u32[]{:S(2)}, u32[]{:S(2)}) async-start(bf16[4,2,15360]{2,1,0:T(2,128)(2,1)} %reshape.1699), calls=%async_computation.12 | async-start | bytes 491520 | tf_op jit(solution)/shard_map/all_to_all | solution.py:96
  572.7 31.3 %all-to-all-start.6 = ((bf16[4,2,15360]{2,1,0:T(2,128)(2,1)}), bf16[4,2,15360]{2,1,0:T(2,128)(2,1)S(1)}, u32[]{:S(2)}, u32[]{:S(2)}) async-start(bf16[4,2,15360]{2,1,0:T(2,128)(2,1)} %reshape.1691), calls=%async_computation.6 | async-start | bytes 491520 | tf_op jit(solution)/shard_map/all_to_all | solution.py:95
  635.5 10.2 %all-to-all-start.7 = ((bf16[8,6,2560]{2,1,0:T(8,128)(2,1)}), bf16[8,6,2560]{2,1,0:T(8,128)(2,1)}, u32[]{:S(2)}, u32[]{:S(2)}) async-start(bf16[8,6,2560]{2,1,0:T(8,128)(2,1)} %reshape.1683), calls=%async_computation.7 | async-start | bytes 655360 | tf_op jit(solution)/shard_map/all_to_all | solution.py:100
  685.6 27.1 %collective-permute-start.3 = (bf16[2,6,10240]{2,0,1:T(2,128)(2,1)S(1)}, bf16[2,6,10240]{2,0,1:T(2,128)(2,1)S(1)}, u32[]{:S(2)}, u32[]{:S(2)}) collective-permute-start(bf16[2,6,10240]{2,0,1:T(2,128)(2,1)S(1)} %add_convert_fusion.2), channel_id=1, source_target_pairs={{8,0},{16,8},{24,16},{9,1},{17,9},{25,17},{10,2},{18,10},{26,18},{... | collective-permute-start | bytes 737288 | tf_op jit(solution)/shard_map/ppermute | solution.py:12
  687.5 24.6 %copy-start.171 = (f32[128,128]{1,0:T(8,128)S(1)}, f32[128,128]{1,0:T(8,128)}, u32[]{:S(2)}) copy-start(f32[128,128]{1,0:T(8,128)} %convolution_bitcast_fusion.15) | copy-start | bytes 196612
  687.5 24.7 %copy-start.168 = (f32[128,128]{1,0:T(8,128)S(1)}, f32[128,128]{1,0:T(8,128)}, u32[]{:S(2)}) copy-start(f32[128,128]{1,0:T(8,128)} %convolution_bitcast_fusion.14) | copy-start | bytes 196612
  687.5 24.7 %copy-start.164 = (f32[128,128]{1,0:T(8,128)S(1)}, f32[128,128]{1,0:T(8,128)}, u32[]{:S(2)}) copy-start(f32[128,128]{1,0:T(8,128)} %convolution_bitcast_fusion.13) | copy-start | bytes 196612
  687.6 24.8 %copy-start.160 = (f32[128,128]{1,0:T(8,128)S(1)}, f32[128,128]{1,0:T(8,128)}, u32[]{:S(2)}) copy-start(f32[128,128]{1,0:T(8,128)} %convolution_bitcast_fusion.12) | copy-start | bytes 196612
  687.6 24.9 %copy-start.156 = (f32[128,128]{1,0:T(8,128)S(1)}, f32[128,128]{1,0:T(8,128)}, u32[]{:S(2)}) copy-start(f32[128,128]{1,0:T(8,128)} %convolution_bitcast_fusion.11) | copy-start | bytes 196612
  687.6 25.0 %copy-start.152 = (f32[128,128]{1,0:T(8,128)S(1)}, f32[128,128]{1,0:T(8,128)}, u32[]{:S(2)}) copy-start(f32[128,128]{1,0:T(8,128)} %convolution_bitcast_fusion.10) | copy-start | bytes 196612
  707.7 23.3 %all-to-all-start.13 = ((bf16[4,2,15360]{2,1,0:T(2,128)(2,1)}), bf16[4,2,15360]{2,1,0:T(2,128)(2,1)S(1)}, u32[]{:S(2)}, u32[]{:S(2)}) async-start(bf16[4,2,15360]{2,1,0:T(2,128)(2,1)} %reshape.1701), calls=%async_computation.13 | async-start | bytes 491520 | tf_op jit(solution)/shard_map/all_to_all | solution.py:96
  731.0 31.1 %all-to-all-start.8 = ((bf16[4,2,15360]{2,1,0:T(2,128)(2,1)}), bf16[4,2,15360]{2,1,0:T(2,128)(2,1)S(1)}, u32[]{:S(2)}, u32[]{:S(2)}) async-start(bf16[4,2,15360]{2,1,0:T(2,128)(2,1)} %reshape.1693), calls=%async_computation.8 | async-start | bytes 491520 | tf_op jit(solution)/shard_map/all_to_all | solution.py:95
  735.9 24.8 %copy-start.122 = (f32[9,64,64]{2,1,0:T(8,128)}, f32[9,64,64]{2,1,0:T(8,128)S(1)}, u32[]{:S(2)}) copy-start(f32[9,64,64]{2,1,0:T(8,128)S(1)} %get-tuple-element.143) | copy-start | bytes 442372
  788.7 9.9 %all-to-all-start.9 = ((bf16[8,6,2560]{2,1,0:T(8,128)(2,1)}), bf16[8,6,2560]{2,1,0:T(8,128)(2,1)S(1)}, u32[]{:S(2)}, u32[]{:S(2)}) async-start(bf16[8,6,2560]{2,1,0:T(8,128)(2,1)} %reshape.1684), calls=%async_computation.9 | async-start | bytes 655360 | tf_op jit(solution)/shard_map/all_to_all | solution.py:100
  793.0 127.7 %all-reduce.17.cloned.1.call-start = ((), (), s32[]{:S(2)}) async-start(), calls=%async_computation.15 | async-start | bytes 589824 | tf_op jit(solution)/shard_map/psum | solution.py:134
  861.3 9.1 all-to-all-start.14
  (151 other events, 1933.2 us)
Sparse Core Ops, SparseCore 0:
  820.6 53.1 all-reduce.16
where the time goes:
time: 944 us; the launch traced here: 930 us
  local copies, waits for them, and re-layouts  609 us (65%)
  matrix products  137 us (15%)
  starting transfers between devices  70 us (7%)
  other arithmetic  49 us (5%)
  blocking collectives  23.7 us (3%)
  waiting for transfers between devices  23.2 us (2%)
  between operations  17.9 us (2%)
    unnamed x379, local copies, waits for them, and re-layouts  229 us
    reshape x105, local copies, waits for them, and re-layouts, split_pixels(): return a.reshape(a.shape[:-1] + (a.shape[-1] // chans, chans))  112 us
    all_to_all x10, local copies, waits for them, and re-layouts, section_backward(): lax.all_to_all(h, 'tm', split_axis=2, concat_axis=0, tiled=True)  61.8 us
    dot_general x45, matrix products, spatial_back(): jnp.einsum('nrpa,nrpb->ab', xpiece, gz_pairs, preferred_element_type=jnp....  54.5 us
    all_to_all x10, local copies, waits for them, and re-layouts, section_backward(): lax.all_to_all(gradient_piece, 'tm', split_axis=2, concat_axis=0, tiled=T...  52.1 us
    convert_element_type x5, local copies, waits for them, and re-layouts, section_backward(): h = (z * sig).astype(jnp.bfloat16)  51.3 us
    select_n x5, local copies, waits for them, and re-layouts, body(): incoming = jnp.where(section_idx == number_sections - 1, top_grad, received)  40.8 us
    dot_general x45, matrix products, spatial_fwd(): jnp.einsum('nrpa,ab->nrpb', piece, paired_kernel(ws[3 * i + j]), preferre...  28.6 us
  transfers between devices with their start and end apart: 20, of which 6 were waited for; matrix products, arithmetic and copies ran while one was open for 48% of the time, Pallas kernels for 0%

commit v1 on v0

--- a/solution.py
+++ b/solution.py
@@ -131,7 +131,7 @@
         grads_in = jnp.where(select, result[None], grads_in)
         if turn + 1 < total_turns:
             received = from_behind(result, "section", -1)
-    sum_spatial, sum_temporal = lax.psum((acc_spatial, acc_temporal), ("tm", "batch"))
+    sum_spatial, sum_temporal = lax.psum(lax.psum((acc_spatial, acc_temporal), "tm"), "batch")
     return (grads_in[None], sum_spatial[None], sum_temporal[None])
 
 

time: 944 us -> 941 us (level)
    psum x1 -> x2, blocking collectives: 23.7 us -> 20.6 us  [the longest x1 16.4 us: body(): lax.psum((acc_spatial, acc_temporal), 'tm')]
  transfers between devices with their start and end apart: 20 -> 21, of which waited for: 6 -> 6; matrix products, arithmetic and copies ran while one was open for 48% -> 48% of each run, Pallas kernels for 0% -> 0%
where the time goes in v1:
time: 941 us; the launch traced here: 926 us
  local copies, waits for them, and re-layouts  609 us (65%)
  matrix products  137 us (15%)
  starting transfers between devices  70.1 us (7%)
  other arithmetic  48.9 us (5%)
  waiting for transfers between devices  22.6 us (2%)
  blocking collectives  20.6 us (2%)
  between operations  17.9 us (2%)
    unnamed x379, local copies, waits for them, and re-layouts  229 us
    reshape x105, local copies, waits for them, and re-layouts, split_pixels(): return a.reshape(a.shape[:-1] + (a.shape[-1] // chans, chans))  112 us
    all_to_all x10, local copies, waits for them, and re-layouts, section_backward(): lax.all_to_all(h, 'tm', split_axis=2, concat_axis=0, tiled=True)  61.8 us
    dot_general x45, matrix products, spatial_back(): jnp.einsum('nrpa,nrpb->ab', xpiece, gz_pairs, preferred_element_type=jnp....  54.6 us
    all_to_all x10, local copies, waits for them, and re-layouts, section_backward(): lax.all_to_all(gradient_piece, 'tm', split_axis=2, concat_axis=0, tiled=T...  52.1 us
    convert_element_type x5, local copies, waits for them, and re-layouts, section_backward(): h = (z * sig).astype(jnp.bfloat16)  51.3 us
    select_n x5, local copies, waits for them, and re-layouts, body(): incoming = jnp.where(section_idx == number_sections - 1, top_grad, received)  40.8 us
    dot_general x45, matrix products, spatial_fwd(): jnp.einsum('nrpa,ab->nrpb', piece, paired_kernel(ws[3 * i + j]), preferre...  28.7 us
  transfers between devices with their start and end apart: 21, of which 6 were waited for; matrix products, arithmetic and copies ran while one was open for 48% of the time, Pallas kernels for 0%

profile of v1, /device:TPU:24, one launch (start us, length us, event | category | flops | bytes accessed | tf_op | source)
XLA Modules:
  0.0 926.0 jit_solution(10682767116544210392)
XLA Ops:
  8.3 8.2 copy.623
  16.5 10.0 %reshape.1685 = bf16[4,2,15360]{2,1,0:T(2,128)(2,1)} reshape(bf16[10240,2,6]{2,1,0:T(2,128)(2,1)} %bitcast.1157) | data formatting | bytes 491520
  26.5 4.2 all-to-all-start
  126.2 13.6 %reshape.1686 = bf16[10240,2,6]{2,1,0:T(2,128)(2,1)} reshape(bf16[4,2,15360]{2,1,0:T(2,128)(2,1)} %all-to-all-done) | data formatting | bytes 491520
  139.9 10.6 %copy.624 = bf16[2,6,4,2560]{3,0,2,1:T(2,128)(2,1)S(1)} copy(bf16[2,6,4,2560]{1,0,3,2:T(2,128)(2,1)} %bitcast.1158) | data formatting | bytes 491520 | tf_op jit(solution)/shard_map/all_to_all | solution.py:95
  153.6 4.3 all-to-all-start.1
  158.9 4.5 all-to-all-done.1
  205.0 10.3 %copy.809 = bf16[2,6,10240]{1,0,2:T(2,128)(2,1)} copy(bf16[2,6,10240]{2,0,1:T(2,128)(2,1)} %get-tuple-element.11) | data formatting | bytes 491520 | tf_op jit(solution)/shard_map/convert_element_type | solution.py:92
  215.3 9.9 %reshape.1695 = bf16[4,2,15360]{2,1,0:T(2,128)(2,1)} reshape(bf16[10240,2,6]{2,1,0:T(2,128)(2,1)} %bitcast.1159) | data formatting | bytes 491520
  233.7 8.2 copy.651
  241.8 9.9 %reshape.1687 = bf16[4,2,15360]{2,1,0:T(2,128)(2,1)} reshape(bf16[10240,2,6]{2,1,0:T(2,128)(2,1)} %bitcast.1173) | data formatting | bytes 491520
  256.8 12.6 %reshape.1696 = bf16[10240,2,6]{2,1,0:T(2,128)(2,1)} reshape(bf16[4,2,15360]{2,1,0:T(2,128)(2,1)S(1)} %all-to-all-done.10) | data formatting | bytes 491520
  269.4 12.2 %copy.902 = bf16[2,6,4,2560]{3,2,0,1:T(4,128)(2,1)S(1)} copy(bf16[2,6,4,2560]{1,0,3,2:T(2,128)(2,1)} %bitcast.1160) | data formatting | bytes 491520 | tf_op jit(solution)/shard_map/all_to_all | solution.py:96
  283.0 12.6 %reshape.1688 = bf16[10240,2,6]{2,1,0:T(2,128)(2,1)} reshape(bf16[4,2,15360]{2,1,0:T(2,128)(2,1)S(1)} %all-to-all-done.2) | data formatting | bytes 491520
  295.6 10.2 %copy.652 = bf16[2,6,4,2560]{3,0,2,1:T(2,128)(2,1)S(1)} copy(bf16[2,6,4,2560]{1,0,3,2:T(2,128)(2,1)} %bitcast.1161) | data formatting | bytes 491520 | tf_op jit(solution)/shard_map/all_to_all | solution.py:95
  314.5 4.4 all-to-all-start.3
  366.2 10.3 %copy.812 = bf16[2,6,10240]{1,0,2:T(2,128)(2,1)} copy(bf16[2,6,10240]{2,0,1:T(2,128)(2,1)} %get-tuple-element.9) | data formatting | bytes 491520 | tf_op jit(solution)/shard_map/convert_element_type | solution.py:92
  376.5 9.9 %reshape.1697 = bf16[4,2,15360]{2,1,0:T(2,128)(2,1)} reshape(bf16[10240,2,6]{2,1,0:T(2,128)(2,1)} %bitcast.1162) | data formatting | bytes 491520
  395.3 8.1 copy.679
  403.5 9.9 %reshape.1689 = bf16[4,2,15360]{2,1,0:T(2,128)(2,1)} reshape(bf16[10240,2,6]{2,1,0:T(2,128)(2,1)} %bitcast.1174) | data formatting | bytes 491520
  418.3 12.6 %reshape.1698 = bf16[10240,2,6]{2,1,0:T(2,128)(2,1)} reshape(bf16[4,2,15360]{2,1,0:T(2,128)(2,1)S(1)} %all-to-all-done.11) | data formatting | bytes 491520
  430.9 12.2 %copy.903 = bf16[2,6,4,2560]{3,2,0,1:T(4,128)(2,1)S(1)} copy(bf16[2,6,4,2560]{1,0,3,2:T(2,128)(2,1)} %bitcast.1163) | data formatting | bytes 491520 | tf_op jit(solution)/shard_map/all_to_all | solution.py:96
  444.5 12.6 %reshape.1690 = bf16[10240,2,6]{2,1,0:T(2,128)(2,1)} reshape(bf16[4,2,15360]{2,1,0:T(2,128)(2,1)S(1)} %all-to-all-done.4) | data formatting | bytes 491520
  457.1 10.2 %copy.680 = bf16[2,6,4,2560]{3,0,2,1:T(2,128)(2,1)S(1)} copy(bf16[2,6,4,2560]{1,0,3,2:T(2,128)(2,1)} %bitcast.1164) | data formatting | bytes 491520 | tf_op jit(solution)/shard_map/all_to_all | solution.py:95
  476.0 4.4 all-to-all-start.5
  525.7 10.3 %copy.815 = bf16[2,6,10240]{1,0,2:T(2,128)(2,1)} copy(bf16[2,6,10240]{2,0,1:T(2,128)(2,1)} %get-tuple-element.7) | data formatting | bytes 491520 | tf_op jit(solution)/shard_map/convert_element_type | solution.py:92
  536.0 9.9 %reshape.1699 = bf16[4,2,15360]{2,1,0:T(2,128)(2,1)} reshape(bf16[10240,2,6]{2,1,0:T(2,128)(2,1)} %bitcast.1165) | data formatting | bytes 491520
  554.7 8.2 copy.707
  562.9 9.9 %reshape.1691 = bf16[4,2,15360]{2,1,0:T(2,128)(2,1)} reshape(bf16[10240,2,6]{2,1,0:T(2,128)(2,1)} %bitcast.1175) | data formatting | bytes 491520
  577.8 12.6 %reshape.1700 = bf16[10240,2,6]{2,1,0:T(2,128)(2,1)} reshape(bf16[4,2,15360]{2,1,0:T(2,128)(2,1)S(1)} %all-to-all-done.12) | data formatting | bytes 491520
  590.5 12.2 %copy.904 = bf16[2,6,4,2560]{3,2,0,1:T(4,128)(2,1)S(1)} copy(bf16[2,6,4,2560]{1,0,3,2:T(2,128)(2,1)} %bitcast.1166) | data formatting | bytes 491520 | tf_op jit(solution)/shard_map/all_to_all | solution.py:96
  604.0 12.6 %reshape.1692 = bf16[10240,2,6]{2,1,0:T(2,128)(2,1)} reshape(bf16[4,2,15360]{2,1,0:T(2,128)(2,1)S(1)} %all-to-all-done.6) | data formatting | bytes 491520
  616.7 10.2 %copy.708 = bf16[2,6,4,2560]{3,0,2,1:T(2,128)(2,1)S(1)} copy(bf16[2,6,4,2560]{1,0,3,2:T(2,128)(2,1)} %bitcast.1167) | data formatting | bytes 491520 | tf_op jit(solution)/shard_map/all_to_all | solution.py:95
  635.5 4.6 all-to-all-start.7
  687.7 10.2 %copy.818 = bf16[2,6,10240]{1,0,2:T(2,128)(2,1)} copy(bf16[2,6,10240]{2,0,1:T(2,128)(2,1)} %get-tuple-element.5) | data formatting | bytes 491520 | tf_op jit(solution)/shard_map/convert_element_type | solution.py:92
  697.9 9.9 %reshape.1701 = bf16[4,2,15360]{2,1,0:T(2,128)(2,1)} reshape(bf16[10240,2,6]{2,1,0:T(2,128)(2,1)} %bitcast.1168) | data formatting | bytes 491520
  713.0 8.1 copy.735
  721.1 9.9 %reshape.1693 = bf16[4,2,15360]{2,1,0:T(2,128)(2,1)} reshape(bf16[10240,2,6]{2,1,0:T(2,128)(2,1)} %bitcast.1176) | data formatting | bytes 491520
  735.9 12.6 %reshape.1702 = bf16[10240,2,6]{2,1,0:T(2,128)(2,1)} reshape(bf16[4,2,15360]{2,1,0:T(2,128)(2,1)S(1)} %all-to-all-done.13) | data formatting | bytes 491520
  748.5 12.2 %copy.905 = bf16[2,6,4,2560]{3,2,0,1:T(4,128)(2,1)S(1)} copy(bf16[2,6,4,2560]{1,0,3,2:T(2,128)(2,1)} %bitcast.1169) | data formatting | bytes 491520 | tf_op jit(solution)/shard_map/all_to_all | solution.py:96
  762.1 12.6 %reshape.1694 = bf16[10240,2,6]{2,1,0:T(2,128)(2,1)} reshape(bf16[4,2,15360]{2,1,0:T(2,128)(2,1)S(1)} %all-to-all-done.8) | data formatting | bytes 491520
  774.7 10.2 %copy.736 = bf16[2,6,4,2560]{3,0,2,1:T(2,128)(2,1)S(1)} copy(bf16[2,6,4,2560]{1,0,3,2:T(2,128)(2,1)} %bitcast.1170) | data formatting | bytes 491520 | tf_op jit(solution)/shard_map/all_to_all | solution.py:95
  788.7 4.3 all-to-all-start.9
  841.1 10.3 %copy.821 = bf16[2,6,10240]{1,0,2:T(2,128)(2,1)} copy(bf16[2,6,10240]{2,0,1:T(2,128)(2,1)} %get-tuple-element.3) | data formatting | bytes 491520 | tf_op jit(solution)/shard_map/convert_element_type | solution.py:92
  851.4 9.9 %reshape.1703 = bf16[4,2,15360]{2,1,0:T(2,128)(2,1)} reshape(bf16[10240,2,6]{2,1,0:T(2,128)(2,1)} %bitcast.1171) | data formatting | bytes 491520
  870.0 12.6 %reshape.1704 = bf16[10240,2,6]{2,1,0:T(2,128)(2,1)} reshape(bf16[4,2,15360]{2,1,0:T(2,128)(2,1)S(1)} %all-to-all-done.14) | data formatting | bytes 491520
  882.7 12.3 %copy.906 = bf16[2,6,4,2560]{3,2,0,1:T(4,128)(2,1)S(1)} copy(bf16[2,6,4,2560]{1,0,3,2:T(2,128)(2,1)} %bitcast.1172) | data formatting | bytes 491520 | tf_op jit(solution)/shard_map/all_to_all | solution.py:96
  896.6 16.4 %psum.30 = f32[3,64,64]{2,1,0:T(8,128)S(1)} all-reduce(f32[3,64,64]{2,1,0:T(8,128)S(1)} %fusion.169), channel_id=1, replica_groups=mesh['section'=4,'tm'=4,'batch'=2] {'tm'}, use_global_device_ids=true, to_apply=%region_2.3 | all-reduce | flops 12288 | bytes 98304 | tf_op jit(solution)/shard_map/psum | solution.py:134
  (816 shorter events, 430.2 us)
Async XLA Ops:
  26.5 99.8 %all-to-all-start = ((bf16[4,2,15360]{2,1,0:T(2,128)(2,1)}), bf16[4,2,15360]{2,1,0:T(2,128)(2,1)}, u32[]{:S(2)}, u32[]{:S(2)}) async-start(bf16[4,2,15360]{2,1,0:T(2,128)(2,1)} %reshape.1685), calls=%async_computation | async-start | bytes 491520 | tf_op jit(solution)/shard_map/all_to_all | solution.py:95
  33.7 160.6 %copy-start.16 = (bf16[128,128,1,1]{1,0,2,3:T(8,128)(2,1)}, bf16[128,128,1,1]{1,0,2,3:T(8,128)(2,1)S(1)}, u32[]{:S(2)}) copy-start(bf16[128,128,1,1]{1,0,2,3:T(8,128)(2,1)S(1)} %reshape.1603) | copy-start | bytes 98308
  33.8 160.7 %copy-start.11 = (bf16[128,128,1,1]{1,0,2,3:T(8,128)(2,1)}, bf16[128,128,1,1]{1,0,2,3:T(8,128)(2,1)S(1)}, u32[]{:S(2)}) copy-start(bf16[128,128,1,1]{1,0,2,3:T(8,128)(2,1)S(1)} %reshape.1604) | copy-start | bytes 98308
  33.9 160.8 %copy-start.6 = (bf16[128,128,1,1]{1,0,2,3:T(8,128)(2,1)}, bf16[128,128,1,1]{1,0,2,3:T(8,128)(2,1)S(1)}, u32[]{:S(2)}) copy-start(bf16[128,128,1,1]{1,0,2,3:T(8,128)(2,1)S(1)} %reshape.1605) | copy-start | bytes 98308
  34.1 162.0 %copy-start.1 = (bf16[128,128,1,1]{1,0,2,3:T(8,128)(2,1)}, bf16[128,128,1,1]{1,0,2,3:T(8,128)(2,1)S(1)}, u32[]{:S(2)}) copy-start(bf16[128,128,1,1]{1,0,2,3:T(8,128)(2,1)S(1)} %reshape.1606) | copy-start | bytes 98308
  34.5 159.6 %copy-start.21 = (bf16[128,128,1,1]{1,0,2,3:T(8,128)(2,1)}, bf16[128,128,1,1]{1,0,2,3:T(8,128)(2,1)S(1)}, u32[]{:S(2)}) copy-start(bf16[128,128,1,1]{1,0,2,3:T(8,128)(2,1)S(1)} %reshape.1602) | copy-start | bytes 98308
  35.6 90.0 %copy-start.43 = (bf16[2,6,80,128]{3,2,0,1:T(8,128)(2,1)}, bf16[2,6,80,128]{3,2,0,1:T(8,128)(2,1)S(1)}, u32[]{:S(2)}) copy-start(bf16[2,6,80,128]{3,2,0,1:T(8,128)(2,1)S(1)} %reshape.1505) | copy-start | bytes 737284
  153.6 9.9 %all-to-all-start.1 = ((bf16[8,6,2560]{2,1,0:T(8,128)(2,1)}), bf16[8,6,2560]{2,1,0:T(8,128)(2,1)S(1)}, u32[]{:S(2)}, u32[]{:S(2)}) async-start(bf16[8,6,2560]{2,1,0:T(8,128)(2,1)} %reshape.1671), calls=%async_computation.1 | async-start | bytes 655360 | tf_op jit(solution)/shard_map/all_to_all | solution.py:100
  202.5 30.9 %collective-permute-start = (bf16[2,6,10240]{2,0,1:T(2,128)(2,1)S(1)}, bf16[2,6,10240]{2,0,1:T(2,128)(2,1)S(1)}, u32[]{:S(2)}, u32[]{:S(2)}) collective-permute-start(bf16[2,6,10240]{2,0,1:T(2,128)(2,1)S(1)} %add_convert_fusion.5), channel_id=1, source_target_pairs={{8,0},{16,8},{24,16},{9,1},{17,9},{25,17},{10,2},{18,10},{26,18},{... | collective-permute-start | bytes 737288 | tf_op jit(solution)/shard_map/ppermute | solution.py:12
  204.9 25.0 %copy-start.162 = (f32[128,128]{1,0:T(8,128)S(1)}, f32[128,128]{1,0:T(8,128)}, u32[]{:S(2)}) copy-start(f32[128,128]{1,0:T(8,128)} %convolution_bitcast_fusion.41) | copy-start | bytes 196612
  204.9 25.7 %copy-start.158 = (f32[128,128]{1,0:T(8,128)S(1)}, f32[128,128]{1,0:T(8,128)}, u32[]{:S(2)}) copy-start(f32[128,128]{1,0:T(8,128)} %convolution_bitcast_fusion.40) | copy-start | bytes 196612
  205.0 26.4 %copy-start.154 = (f32[128,128]{1,0:T(8,128)S(1)}, f32[128,128]{1,0:T(8,128)}, u32[]{:S(2)}) copy-start(f32[128,128]{1,0:T(8,128)} %convolution_bitcast_fusion.39) | copy-start | bytes 196612
  205.0 27.0 %copy-start.150 = (f32[128,128]{1,0:T(8,128)S(1)}, f32[128,128]{1,0:T(8,128)}, u32[]{:S(2)}) copy-start(f32[128,128]{1,0:T(8,128)} %convolution_bitcast_fusion.38) | copy-start | bytes 196612
  205.0 27.7 %copy-start.149 = (f32[128,128]{1,0:T(8,128)S(1)}, f32[128,128]{1,0:T(8,128)}, u32[]{:S(2)}) copy-start(f32[128,128]{1,0:T(8,128)} %convolution_bitcast_fusion.37) | copy-start | bytes 196612
  225.2 26.6 %all-to-all-start.10 = ((bf16[4,2,15360]{2,1,0:T(2,128)(2,1)}), bf16[4,2,15360]{2,1,0:T(2,128)(2,1)S(1)}, u32[]{:S(2)}, u32[]{:S(2)}) async-start(bf16[4,2,15360]{2,1,0:T(2,128)(2,1)} %reshape.1695), calls=%async_computation.10 | async-start | bytes 491520 | tf_op jit(solution)/shard_map/all_to_all | solution.py:96
  251.7 31.3 %all-to-all-start.2 = ((bf16[4,2,15360]{2,1,0:T(2,128)(2,1)}), bf16[4,2,15360]{2,1,0:T(2,128)(2,1)S(1)}, u32[]{:S(2)}, u32[]{:S(2)}) async-start(bf16[4,2,15360]{2,1,0:T(2,128)(2,1)} %reshape.1687), calls=%async_computation.2 | async-start | bytes 491520 | tf_op jit(solution)/shard_map/all_to_all | solution.py:95
  314.5 10.0 %all-to-all-start.3 = ((bf16[8,6,2560]{2,1,0:T(8,128)(2,1)}), bf16[8,6,2560]{2,1,0:T(8,128)(2,1)}, u32[]{:S(2)}, u32[]{:S(2)}) async-start(bf16[8,6,2560]{2,1,0:T(8,128)(2,1)} %reshape.1681), calls=%async_computation.3 | async-start | bytes 655360 | tf_op jit(solution)/shard_map/all_to_all | solution.py:100
  363.7 31.3 %collective-permute-start.1 = (bf16[2,6,10240]{2,0,1:T(2,128)(2,1)S(1)}, bf16[2,6,10240]{2,0,1:T(2,128)(2,1)S(1)}, u32[]{:S(2)}, u32[]{:S(2)}) collective-permute-start(bf16[2,6,10240]{2,0,1:T(2,128)(2,1)S(1)} %add_convert_fusion.4), channel_id=1, source_target_pairs={{8,0},{16,8},{24,16},{9,1},{17,9},{25,17},{10,2},{18,10},{26,18},{... | collective-permute-start | bytes 737288 | tf_op jit(solution)/shard_map/ppermute | solution.py:12
  366.2 25.4 %copy-start.167 = (f32[128,128]{1,0:T(8,128)S(1)}, f32[128,128]{1,0:T(8,128)}, u32[]{:S(2)}) copy-start(f32[128,128]{1,0:T(8,128)} %convolution_bitcast_fusion.32) | copy-start | bytes 196612
  366.2 26.1 %copy-start.163 = (f32[128,128]{1,0:T(8,128)S(1)}, f32[128,128]{1,0:T(8,128)}, u32[]{:S(2)}) copy-start(f32[128,128]{1,0:T(8,128)} %convolution_bitcast_fusion.31) | copy-start | bytes 196612
  366.2 26.8 %copy-start.159 = (f32[128,128]{1,0:T(8,128)S(1)}, f32[128,128]{1,0:T(8,128)}, u32[]{:S(2)}) copy-start(f32[128,128]{1,0:T(8,128)} %convolution_bitcast_fusion.30) | copy-start | bytes 196612
  366.2 27.5 %copy-start.155 = (f32[128,128]{1,0:T(8,128)S(1)}, f32[128,128]{1,0:T(8,128)}, u32[]{:S(2)}) copy-start(f32[128,128]{1,0:T(8,128)} %convolution_bitcast_fusion.29) | copy-start | bytes 196612
  366.2 28.2 %copy-start.151 = (f32[128,128]{1,0:T(8,128)S(1)}, f32[128,128]{1,0:T(8,128)}, u32[]{:S(2)}) copy-start(f32[128,128]{1,0:T(8,128)} %convolution_bitcast_fusion.28) | copy-start | bytes 196612
  386.4 27.0 %all-to-all-start.11 = ((bf16[4,2,15360]{2,1,0:T(2,128)(2,1)}), bf16[4,2,15360]{2,1,0:T(2,128)(2,1)S(1)}, u32[]{:S(2)}, u32[]{:S(2)}) async-start(bf16[4,2,15360]{2,1,0:T(2,128)(2,1)} %reshape.1697), calls=%async_computation.11 | async-start | bytes 491520 | tf_op jit(solution)/shard_map/all_to_all | solution.py:96
  413.4 31.1 %all-to-all-start.4 = ((bf16[4,2,15360]{2,1,0:T(2,128)(2,1)}), bf16[4,2,15360]{2,1,0:T(2,128)(2,1)S(1)}, u32[]{:S(2)}, u32[]{:S(2)}) async-start(bf16[4,2,15360]{2,1,0:T(2,128)(2,1)} %reshape.1689), calls=%async_computation.4 | async-start | bytes 491520 | tf_op jit(solution)/shard_map/all_to_all | solution.py:95
  476.0 10.0 %all-to-all-start.5 = ((bf16[8,6,2560]{2,1,0:T(8,128)(2,1)}), bf16[8,6,2560]{2,1,0:T(8,128)(2,1)}, u32[]{:S(2)}, u32[]{:S(2)}) async-start(bf16[8,6,2560]{2,1,0:T(8,128)(2,1)} %reshape.1682), calls=%async_computation.5 | async-start | bytes 655360 | tf_op jit(solution)/shard_map/all_to_all | solution.py:100
  523.5 30.9 %collective-permute-start.2 = (bf16[2,6,10240]{2,0,1:T(2,128)(2,1)S(1)}, bf16[2,6,10240]{2,0,1:T(2,128)(2,1)S(1)}, u32[]{:S(2)}, u32[]{:S(2)}) collective-permute-start(bf16[2,6,10240]{2,0,1:T(2,128)(2,1)S(1)} %add_convert_fusion.3), channel_id=1, source_target_pairs={{8,0},{16,8},{24,16},{9,1},{17,9},{25,17},{10,2},{18,10},{26,18},{... | collective-permute-start | bytes 737288 | tf_op jit(solution)/shard_map/ppermute | solution.py:12
  525.7 25.2 %copy-start.169 = (f32[128,128]{1,0:T(8,128)S(1)}, f32[128,128]{1,0:T(8,128)}, u32[]{:S(2)}) copy-start(f32[128,128]{1,0:T(8,128)} %convolution_bitcast_fusion.23) | copy-start | bytes 196612
  525.7 25.9 %copy-start.165 = (f32[128,128]{1,0:T(8,128)S(1)}, f32[128,128]{1,0:T(8,128)}, u32[]{:S(2)}) copy-start(f32[128,128]{1,0:T(8,128)} %convolution_bitcast_fusion.22) | copy-start | bytes 196612
  525.7 26.6 %copy-start.161 = (f32[128,128]{1,0:T(8,128)S(1)}, f32[128,128]{1,0:T(8,128)}, u32[]{:S(2)}) copy-start(f32[128,128]{1,0:T(8,128)} %convolution_bitcast_fusion.21) | copy-start | bytes 196612
  525.7 27.3 %copy-start.157 = (f32[128,128]{1,0:T(8,128)S(1)}, f32[128,128]{1,0:T(8,128)}, u32[]{:S(2)}) copy-start(f32[128,128]{1,0:T(8,128)} %convolution_bitcast_fusion.20) | copy-start | bytes 196612
  525.7 28.0 %copy-start.153 = (f32[128,128]{1,0:T(8,128)S(1)}, f32[128,128]{1,0:T(8,128)}, u32[]{:S(2)}) copy-start(f32[128,128]{1,0:T(8,128)} %convolution_bitcast_fusion.19) | copy-start | bytes 196612
  545.9 26.9 %all-to-all-start.12 = ((bf16[4,2,15360]{2,1,0:T(2,128)(2,1)}), bf16[4,2,15360]{2,1,0:T(2,128)(2,1)S(1)}, u32[]{:S(2)}, u32[]{:S(2)}) async-start(bf16[4,2,15360]{2,1,0:T(2,128)(2,1)} %reshape.1699), calls=%async_computation.12 | async-start | bytes 491520 | tf_op jit(solution)/shard_map/all_to_all | solution.py:96
  572.8 31.3 %all-to-all-start.6 = ((bf16[4,2,15360]{2,1,0:T(2,128)(2,1)}), bf16[4,2,15360]{2,1,0:T(2,128)(2,1)S(1)}, u32[]{:S(2)}, u32[]{:S(2)}) async-start(bf16[4,2,15360]{2,1,0:T(2,128)(2,1)} %reshape.1691), calls=%async_computation.6 | async-start | bytes 491520 | tf_op jit(solution)/shard_map/all_to_all | solution.py:95
  635.5 10.2 %all-to-all-start.7 = ((bf16[8,6,2560]{2,1,0:T(8,128)(2,1)}), bf16[8,6,2560]{2,1,0:T(8,128)(2,1)}, u32[]{:S(2)}, u32[]{:S(2)}) async-start(bf16[8,6,2560]{2,1,0:T(8,128)(2,1)} %reshape.1683), calls=%async_computation.7 | async-start | bytes 655360 | tf_op jit(solution)/shard_map/all_to_all | solution.py:100
  685.7 27.0 %collective-permute-start.3 = (bf16[2,6,10240]{2,0,1:T(2,128)(2,1)S(1)}, bf16[2,6,10240]{2,0,1:T(2,128)(2,1)S(1)}, u32[]{:S(2)}, u32[]{:S(2)}) collective-permute-start(bf16[2,6,10240]{2,0,1:T(2,128)(2,1)S(1)} %add_convert_fusion.2), channel_id=1, source_target_pairs={{8,0},{16,8},{24,16},{9,1},{17,9},{25,17},{10,2},{18,10},{26,18},{... | collective-permute-start | bytes 737288 | tf_op jit(solution)/shard_map/ppermute | solution.py:12
  687.6 24.6 %copy-start.168 = (f32[128,128]{1,0:T(8,128)S(1)}, f32[128,128]{1,0:T(8,128)}, u32[]{:S(2)}) copy-start(f32[128,128]{1,0:T(8,128)} %convolution_bitcast_fusion.14) | copy-start | bytes 196612
  687.7 24.7 %copy-start.164 = (f32[128,128]{1,0:T(8,128)S(1)}, f32[128,128]{1,0:T(8,128)}, u32[]{:S(2)}) copy-start(f32[128,128]{1,0:T(8,128)} %convolution_bitcast_fusion.13) | copy-start | bytes 196612
  687.7 24.8 %copy-start.160 = (f32[128,128]{1,0:T(8,128)S(1)}, f32[128,128]{1,0:T(8,128)}, u32[]{:S(2)}) copy-start(f32[128,128]{1,0:T(8,128)} %convolution_bitcast_fusion.12) | copy-start | bytes 196612
  687.7 24.9 %copy-start.156 = (f32[128,128]{1,0:T(8,128)S(1)}, f32[128,128]{1,0:T(8,128)}, u32[]{:S(2)}) copy-start(f32[128,128]{1,0:T(8,128)} %convolution_bitcast_fusion.11) | copy-start | bytes 196612
  687.7 24.9 %copy-start.152 = (f32[128,128]{1,0:T(8,128)S(1)}, f32[128,128]{1,0:T(8,128)}, u32[]{:S(2)}) copy-start(f32[128,128]{1,0:T(8,128)} %convolution_bitcast_fusion.10) | copy-start | bytes 196612
  707.8 23.2 %all-to-all-start.13 = ((bf16[4,2,15360]{2,1,0:T(2,128)(2,1)}), bf16[4,2,15360]{2,1,0:T(2,128)(2,1)S(1)}, u32[]{:S(2)}, u32[]{:S(2)}) async-start(bf16[4,2,15360]{2,1,0:T(2,128)(2,1)} %reshape.1701), calls=%async_computation.13 | async-start | bytes 491520 | tf_op jit(solution)/shard_map/all_to_all | solution.py:96
  731.0 31.1 %all-to-all-start.8 = ((bf16[4,2,15360]{2,1,0:T(2,128)(2,1)}), bf16[4,2,15360]{2,1,0:T(2,128)(2,1)S(1)}, u32[]{:S(2)}, u32[]{:S(2)}) async-start(bf16[4,2,15360]{2,1,0:T(2,128)(2,1)} %reshape.1693), calls=%async_computation.8 | async-start | bytes 491520 | tf_op jit(solution)/shard_map/all_to_all | solution.py:95
  735.9 24.8 %copy-start.122 = (f32[9,64,64]{2,1,0:T(8,128)}, f32[9,64,64]{2,1,0:T(8,128)S(1)}, u32[]{:S(2)}) copy-start(f32[9,64,64]{2,1,0:T(8,128)S(1)} %get-tuple-element.143) | copy-start | bytes 442372
  788.7 9.9 %all-to-all-start.9 = ((bf16[8,6,2560]{2,1,0:T(8,128)(2,1)}), bf16[8,6,2560]{2,1,0:T(8,128)(2,1)S(1)}, u32[]{:S(2)}, u32[]{:S(2)}) async-start(bf16[8,6,2560]{2,1,0:T(8,128)(2,1)} %reshape.1684), calls=%async_computation.9 | async-start | bytes 655360 | tf_op jit(solution)/shard_map/all_to_all | solution.py:100
  793.0 73.8 %all-reduce.18.cloned.1.call-start = ((), (), s32[]{:S(2)}) async-start(), calls=%async_computation.15 | async-start | bytes 589824 | tf_op jit(solution)/shard_map/psum | solution.py:134
  861.3 8.7 all-to-all-start.14
  864.7 52.5 %all-reduce.20.cloned.1.call-start = ((), (), s32[]{:S(2)}) async-start(), calls=%async_computation.16 | async-start | bytes 589824 | tf_op jit(solution)/shard_map/psum | solution.py:134
  (152 other events, 1958.6 us)
Sparse Core Ops, SparseCore 0:
  820.6 43.2 all-reduce.17
  868.0 19.9 all-reduce.19
